TPU v7x, 128 devices: a whole 4x4x4 slice. The times are simulated.
128 devices in a mesh: crop: 2 (over x_hi), row: 16 (over z, y), col: 4 (over x_lo, core).
Axes of the slice: x: 4 (x_hi: 2, x_lo: 2; x = x_hi * 2 + x_lo), y: 4, z: 4, core: 2. Of those that a mesh axis runs over, the one named last changes fastest.
Arguments:
- pair_state: bfloat16 [1024, 512, 128], P(('crop', 'row'), 'col'), parts along dimension 0, may hold values from -6 to 6
- valid_tokens: int32 [2], P('crop'), parts along dimension 0, may hold values from 256 to 512
- w_query: bfloat16 [128, 128], replicated, may hold values from -2 to 2
- w_key: bfloat16 [128, 128], replicated, may hold values from -2 to 2
- w_value: bfloat16 [128, 128], replicated, may hold values from -0.5 to 0.5
- w_gate: bfloat16 [128, 128], replicated, may hold values from -0.5 to 0.5
- b_gate: float32 [128], replicated, may hold values from -4 to 4
- w_bias: bfloat16 [128, 4], replicated, may hold values from -0.5 to 0.5
- w_out: bfloat16 [128, 128], replicated, may hold values from -0.5 to 0.5
- b_out: float32 [128], replicated, may hold values from -3 to 3
Outputs:
- pair_out: bfloat16 [1024, 512, 128], P(('crop', 'row'), 'col'), parts along dimension 0
There are 2 independent parts, one for each index of `crop`. A program takes and returns all parts, laid end to end along the dimension named above; an argument that names none is the same for every part. Nothing has to cross between parts.
Inputs may be any that keep to these rules, and one draw needn't show every extreme that they name: `valid_tokens`: number of tokens of the crop that are real; the others are padding.
All inputs are finite; a program needn't handle non-finite values.
Results may differ from a plain program's by a relative error of at most 0.0055.
Values may be sent and summed in bfloat16 or wider, within the bound.
No kernel may reach another device: no remote copies, remote signals or barrier semaphores. Data moves between devices by JAX's collectives and lax.ppermute only.
A program may use at most 256 MiB of HBM per device.

v0:
```python
import functools

import jax
import jax.numpy as jnp
from jax import lax
from jax.experimental import pallas as pl
from jax.experimental.pallas import tpu as pltpu
from jax.sharding import Mesh
from jax.sharding import PartitionSpec as P

F32 = jnp.float32
BF16 = jnp.bfloat16
MASKED_SCORE = -1000000000.0
CONTRACT_LAST = (((1,), (1,)), ((), ()))
MICROSECOND = 1_150_000_000
ORDER = (10, 5, 0, 1, 9, 4, 6, 2, 3, 15, 11, 7, 12, 8, 13, 14)
ORDER_BACK = (10, 14, 5, 1, 9, 2, 3, 11, 13, 7, 8, 4, 0, 6, 15, 12)
PLACE = tuple(ORDER.index(row) for row in range(len(ORDER)))
PLACE_BACK = tuple(ORDER_BACK.index(row) for row in range(len(ORDER)))
WHOLE = pl.BlockSpec(memory_space=pltpu.VMEM)
SCALARS = pl.BlockSpec(memory_space=pltpu.SMEM)


def normalize(floats):
    average = jnp.mean(floats, axis=-1, keepdims=True)
    centered = floats - average
    variance = jnp.mean(centered * centered, axis=-1, keepdims=True)
    return (centered * lax.rsqrt(variance + 1e-05)).astype(BF16)


def pack_kernel(x_ref, wb_ref, out_ref):
    rows = x_ref.shape[0]
    peers, slots = out_ref.shape[:2]
    heads = wb_ref.shape[0]
    picks = slots - heads
    cols = x_ref.shape[1]
    normed = normalize(x_ref[...].reshape(rows * cols, -1).astype(F32))
    bias = lax.dot_general(wb_ref[...], normed, CONTRACT_LAST, preferred_element_type=F32)
    bias = jnp.stack([bias[:, r * cols : (r + 1) * cols] for r in range(rows)], axis=1)
    bias = bias.astype(BF16)
    for d in range(peers):
        out_ref[d, picks:] = bias
    turned = jnp.swapaxes(x_ref[...], 0, 1)
    for q in range(picks):
        out_ref[:, q] = turned[q * peers : (q + 1) * peers]


def bias_kernel(info_ref, got_ref, out_ref):
    heads, width, tokens = out_ref.shape
    first = got_ref.shape[1] - heads
    key_ok = lax.broadcasted_iota(jnp.int32, (1, tokens), 1) < info_ref[3]
    for h in range(heads):
        block = jnp.concatenate([got_ref[at, first + h] for at in PLACE], axis=0).astype(F32)
        out_ref[h] = jnp.where(key_ok, jnp.transpose(block), MASKED_SCORE).astype(BF16)


def column_is_real(info_ref, q, peers, width):
    column = (info_ref[1] * 2 + info_ref[0]) * width + q * peers + info_ref[2]
    return column < info_ref[3]


def project_kernel(
    info_ref, got_ref, wq_ref, wk_ref, wv_ref, wg_ref, bg_ref, qkv_ref, gate_ref, *, head_size
):
    rows, _, tile_rows, channels = got_ref.shape
    picks, tokens = qkv_ref.shape[:2]
    group = picks // 2
    weights_in = jnp.concatenate([wq_ref[...], wk_ref[...], wv_ref[...], wg_ref[...]], axis=1)
    for first in range(0, picks, group):
        mine = jnp.concatenate(
            [got_ref[at, first + q] for q in range(group) for at in PLACE], axis=0
        ).astype(F32)
        projected = jnp.dot(normalize(mine), weights_in, preferred_element_type=F32)
        for q in range(group):
            real = column_is_real(info_ref, first + q, rows, rows * picks)
            scale = jnp.where(real, F32(head_size ** (-0.5)), F32(0.0))
            part = projected[q * tokens : (q + 1) * tokens]
            qkv_ref[first + q, :, :channels] = (part[:, :channels] * scale).astype(BF16)
            qkv_ref[first + q, :, channels:] = part[:, channels : 3 * channels].astype(BF16)
            gate_ref[first + q] = jax.nn.sigmoid(part[:, 3 * channels :] + bg_ref[...])


def attend_kernel(info_ref, got_ref, qkv_ref, gate_ref, wo_ref, bo_ref, *refs, far):
    blocks, out_ref, bias_s = refs[:-2], refs[-2], refs[-1]
    core, pair = info_ref[0], info_ref[1]
    earlier, blocks = (blocks[:2], blocks[2:]) if far == 2 else ((), blocks)
    rows, _, tile_rows, channels = got_ref.shape
    picks, tokens = qkv_ref.shape[:2]
    heads, width = blocks[0].shape[:2]
    head_size = channels // heads
    tiles = width // tile_rows
    half = 1 - pair if far else pair
    bias_s[heads] = jnp.zeros(bias_s.shape[1:], F32)
    starts = []
    for n, block in enumerate(blocks):
        for h in range(heads):
            bias_s[h, n * width : (n + 1) * width] = block[h].astype(F32)
        mine = core if (n == 0) == (far != 2) else 1 - core
        starts.append((half * 2 + mine) * width)
    lane_head = lax.broadcasted_iota(jnp.int32, (1, channels), 1) // head_size
    for n, start in enumerate(starts):
        at = pl.ds(pl.multiple_of(start, width), width)
        attended = []
        for q in range(picks):
            real = column_is_real(info_ref, q, rows, width)
            some = qkv_ref[q, at, :channels]
            keys = qkv_ref[q, :, channels : 2 * channels]
            values = qkv_ref[q, :, 2 * channels :]
            values_ones = jnp.concatenate([values, jnp.ones_like(values)], axis=1)
            stacked = jnp.concatenate(
                [jnp.where(lane_head == h, some, jnp.zeros_like(some)) for h in range(heads)],
                axis=0,
            )
            bias = jnp.concatenate(
                [
                    bias_s[jnp.where(real, h, heads), n * width : (n + 1) * width]
                    for h in range(heads)
                ],
                axis=0,
            )
            scores = lax.dot_general(stacked, keys, CONTRACT_LAST, preferred_element_type=F32)
            scores = scores + bias
            weights = jnp.exp(scores - jnp.max(scores, axis=1, keepdims=True)).astype(BF16)
            both = jnp.dot(weights, values_ones, preferred_element_type=F32)
            top = total = None
            for h in range(heads):
                one = both[h * width : (h + 1) * width]
                if h == 0:
                    top, total = one[:, :channels], one[:, channels:]
                else:
                    top = jnp.where(lane_head == h, one[:, :channels], top)
                    total = jnp.where(lane_head == h, one[:, channels:], total)
            attended.append(gate_ref[q, at] * (top / total))
        mix = jnp.concatenate(attended, axis=0).astype(BF16)
        update = jnp.dot(mix, wo_ref[...], preferred_element_type=F32) + bo_ref[...]
        for t in range(tiles):
            place = info_ref[4 + start // tile_rows + t]
            to = info_ref[4 + rows + start // tile_rows + t] if earlier else n * tiles + t
            for q in range(picks):
                change = update[q * width + t * tile_rows : q * width + (t + 1) * tile_rows]
                out_ref[to, q] = (got_ref[place, q].astype(F32) + change).astype(BF16)
    if earlier:
        near_ref, far_ref = earlier
        for part, first, half_of, mine in (
            (near_ref, 0, pair, core),
            (near_ref, tiles, pair, 1 - core),
            (far_ref, 0, half, core),
        ):
            for t in range(tiles):
                to = info_ref[4 + rows + (half_of * 2 + mine) * tiles + t]
                out_ref[to] = part[first + t]


def unpack_kernel(got_ref, out_ref):
    peers, picks = got_ref.shape[:2]
    for q in range(picks):
        columns = jnp.stack([got_ref[PLACE_BACK[row], q] for row in ORDER], axis=0)
        out_ref[:, q * peers : (q + 1) * peers] = jnp.swapaxes(columns, 0, 1)


def call(kernel, name, out, *operands, cost, vmem=28, scratch=(), **grid):
    grid.setdefault("in_specs", [SCALARS if o.ndim == 1 else WHOLE for o in operands])
    grid.setdefault("out_specs", jax.tree.map(lambda _: WHOLE, out))
    return pl.pallas_call(
        kernel,
        out_shape=out,
        scratch_shapes=list(scratch),
        compiler_params=pltpu.CompilerParams(vmem_limit_bytes=vmem << 20),
        cost_estimate=pl.CostEstimate(flops=cost, bytes_accessed=0, transcendentals=0),
        name=name,
        **grid,
    )(*operands)


def local(pair_state, valid_tokens, w_query, w_key, w_value, w_gate, b_gate, w_bias, w_out, b_out):
    tile_rows, tile_cols, channels = pair_state.shape
    heads = w_bias.shape[1]
    peers = lax.axis_size("row")
    picks = tile_cols // peers
    tokens = peers * tile_rows
    places = jnp.array(PLACE + PLACE_BACK, jnp.int32)
    here = [lax.axis_index("core"), lax.axis_index("xl"), places[lax.axis_index("row")]]
    info = jnp.concatenate([jnp.stack(here + [valid_tokens[0]]).astype(jnp.int32), places])
    of = jax.ShapeDtypeStruct
    swap = [(0, 1), (1, 0)]

    def exchange(array, order):
        return lax.all_to_all(array, "row", 0, 0, axis_index_groups=[list(order)], tiled=True)

    part = tile_rows // 2
    slots = picks + heads
    sent = call(
        pack_kernel, "pack", of((peers, slots, tile_rows, channels), BF16), pair_state, w_bias.T,
        grid=(2,),
        in_specs=[
            pl.BlockSpec((part, tile_cols, channels), lambda a: (a, 0, 0)),
            pl.BlockSpec((heads, channels), lambda a: (0, 0)),
        ],
        out_specs=pl.BlockSpec((peers, slots, part, channels), lambda a: (0, 0, a, 0)),
        cost=4 * MICROSECOND, vmem=62,
    )
    got = exchange(sent, ORDER)
    own = call(bias_kernel, "turn_bias", of((heads, tile_cols, tokens), BF16), info, got, cost=MICROSECOND)
    far = lax.ppermute(own, "xl", swap)
    near = lax.ppermute(own, "core", swap)
    qkv, gate = call(
        functools.partial(project_kernel, head_size=channels // heads), "project",
        (of((picks, tokens, 3 * channels), BF16), of((picks, tokens, channels), F32)),
        info, got, w_query, w_key, w_value, w_gate, b_gate[None],
        cost=3 * MICROSECOND,
    )

    def attend(name, far, *blocks, earlier=()):
        count = len(blocks)
        tiles = peers if earlier else count * tile_cols // tile_rows
        return call(
            functools.partial(attend_kernel, far=far), name,
            of((tiles, picks, tile_rows, channels), BF16),
            info, got, qkv, gate, w_out, b_out[None], *earlier, *blocks,
            cost=3 * count * MICROSECOND,
            scratch=[pltpu.VMEM((heads + 1, count * tile_cols, tokens), F32)],
        )

    first = attend("attend_near", 0, own, near)
    far, first = lax.optimization_barrier((far, first))
    last = lax.ppermute(far, "core", swap)
    second = attend("attend_far", 1, far)
    done = attend("attend_last", 2, last, earlier=(first, second))
    back = exchange(done, ORDER_BACK)
    return call(unpack_kernel, "unpack", of(pair_state.shape, BF16), back, cost=MICROSECOND)


def solution(mesh):
    crops, rows, cols = (mesh.shape[name] for name in ("crop", "row", "col"))
    split = Mesh(
        mesh.devices.reshape(crops, rows, cols // 2, 2), ("crop", "row", "xl", "core")
    )
    return jax.shard_map(
        local,
        mesh=split,
        in_specs=(P(("crop", "row"), ("xl", "core"), None), P("crop")) + (P(),) * 8,
        out_specs=P(("crop", "row"), ("xl", "core"), None),
        check_vma=False,
    )
```

profile of v0, /device:TPU:0, one launch (start us, length us, event | category | flops | bytes accessed | tf_op | source)
XLA Modules:
  0.0 77.0 jit_solution(18140550569614817636)
XLA Ops:
  0.0 3.8 %pack.1 = bf16[16,12,32,128]{3,2,1,0:T(8,128)(2,1)} custom-call(bf16[32,128,128]{2,1,0:T(8,128)(2,1)} %x_ref.1, bf16[4,128]{1,0:T(4,128)(2,1)} %bitcast.9), custom_call_target="tpu_custom_call" | custom-call | flops 4600000000 | tf_op jit(solution)/shard_map/pack/pallas_call | solution.py:164
  3.8 0.0 copy-start.7
  3.8 10.4 %all-to-all-start = ((bf16[16,12,32,128]{3,2,1,0:T(8,128)(2,1)}), bf16[16,12,32,128]{3,2,1,0:T(8,128)(2,1)S(1)}, u32[]{:S(2)}, u32[]{:S(2)}) async-start(bf16[16,12,32,128]{3,2,1,0:T(8,128)(2,1)} %pack.1), calls=%async_computation | async-start | bytes 3145728 | tf_op jit(solution)/shard_map/all_to_all | solution.py:188
  14.8 0.0 copy-done.7
  14.8 0.6 dynamic_slice.3
  15.4 0.7 concatenate.3.info_ref
  16.1 0.0 copy-start
  16.1 0.0 copy-start.1
  16.1 0.0 copy-start.2
  16.1 0.0 copy-start.3
  16.1 0.0 copy-start.5
  16.1 17.1 %all-to-all-done.got_ref = bf16[16,12,32,128]{3,2,1,0:T(8,128)(2,1)S(1)} async-done(((bf16[16,12,32,128]{3,2,1,0:T(8,128)(2,1)}), bf16[16,12,32,128]{3,2,1,0:T(8,128)(2,1)S(1)}, u32[]{:S(2)}, u32[]{:S(2)}) %all-to-all-start) | async-done | bytes 1572896 | tf_op jit(solution)/shard_map/all_to_all | solution.py:188
  33.2 0.7 turn_bias.1.refs_0_
  33.9 0.1 collective-permute-start.1
  34.0 1.6 %collective-permute-start = (bf16[4,128,512]{2,1,0:T(8,128)(2,1)S(1)}, bf16[4,128,512]{2,1,0:T(8,128)(2,1)S(1)}, u32[]{:S(2)}, u32[]{:S(2)}) collective-permute-start(bf16[4,128,512]{2,1,0:T(8,128)(2,1)S(1)} %turn_bias.1.refs_0_), channel_id=1, source_target_pairs={{0,2},{2,0},{1,3},{3,1},{4,6},{6,4},{5,7},{7,5},{8,10},{10,8},{9,1... | collective-permute-start | bytes 1572872 | tf_op jit(solution)/shard_map/ppermute | solution.py:204
  35.6 0.0 copy-done
  35.6 0.0 copy-done.1
  35.6 0.0 copy-done.2
  35.6 0.0 copy-done.3
  35.6 0.0 copy-done.5
  35.6 0.0 copy-start.4
  35.6 0.0 copy-start.6
  35.6 3.4 %project.1 = (bf16[8,512,384]{2,1,0:T(8,128)(2,1)S(1)}, f32[8,512,128]{2,1,0:T(8,128)S(1)}) custom-call(s32[36]{0:T(128)S(1)} %concatenate.3.info_ref, bf16[16,12,32,128]{3,2,1,0:T(8,128)(2,1)S(1)} %all-to-all-done.got_ref, bf16[128,128]{1,0:T(8,128)(2,1)S(1)} %copy-done, bf16[128,128]{1,0:T(8,128)(2,1)S(1)} %copy-done.1, bf16[128,128]{1,0:T(8,128)(2,1)S(1)} %copy-done.2, ...), custom_call_target="tpu_custom_call" | custom-call | flops 3449999872 | tf_op jit(solution)/shard_map/project/pallas_call | solution.py:164
  39.0 0.0 collective-permute-done.1.refs_1_
  39.0 0.0 copy-done.4
  39.0 0.0 copy-done.6
  39.0 6.3 %attend_near.1.refs_0_ = bf16[8,8,32,128]{3,2,1,0:T(8,128)(2,1)S(1)} custom-call(s32[36]{0:T(128)S(1)} %concatenate.3.info_ref, bf16[16,12,32,128]{3,2,1,0:T(8,128)(2,1)S(1)} %all-to-all-done.got_ref, bf16[8,512,384]{2,1,0:T(8,128)(2,1)S(1)} %get-tuple-element.9.qkv_ref, f32[8,512,128]{2,1,0:T(8,128)S(1)} %get-tuple-element.10.gate_ref, ...), custom_call_target="tpu_custom_call" | custom-call | flops 6899999744 | tf_op jit(solution)/shard_map/attend_near/pallas_call | solution.py:164
  45.3 3.0 %collective-permute-done.refs_0_ = bf16[4,128,512]{2,1,0:T(8,128)(2,1)S(1)} collective-permute-done((bf16[4,128,512]{2,1,0:T(8,128)(2,1)S(1)}, bf16[4,128,512]{2,1,0:T(8,128)(2,1)S(1)}, u32[]{:S(2)}, u32[]{:S(2)}) %collective-permute-start) | collective-permute-done | bytes 524320 | tf_op jit(solution)/shard_map/ppermute | solution.py:204
  48.4 0.0 collective-permute-start.2
  48.4 3.6 %attend_far.1.refs_1_ = bf16[4,8,32,128]{3,2,1,0:T(8,128)(2,1)S(1)} custom-call(s32[36]{0:T(128)S(1)} %concatenate.3.info_ref, bf16[16,12,32,128]{3,2,1,0:T(8,128)(2,1)S(1)} %all-to-all-done.got_ref, bf16[8,512,384]{2,1,0:T(8,128)(2,1)S(1)} %get-tuple-element.9.qkv_ref, f32[8,512,128]{2,1,0:T(8,128)S(1)} %get-tuple-element.10.gate_ref, ...), custom_call_target="tpu_custom_call" | custom-call | flops 3449999872 | tf_op jit(solution)/shard_map/attend_far/pallas_call | solution.py:164
  51.9 0.0 collective-permute-done.2.refs_2_
  51.9 3.6 %attend_last.1 = bf16[16,8,32,128]{3,2,1,0:T(8,128)(2,1)S(1)} custom-call(s32[36]{0:T(128)S(1)} %concatenate.3.info_ref, bf16[16,12,32,128]{3,2,1,0:T(8,128)(2,1)S(1)} %all-to-all-done.got_ref, bf16[8,512,384]{2,1,0:T(8,128)(2,1)S(1)} %get-tuple-element.9.qkv_ref, f32[8,512,128]{2,1,0:T(8,128)S(1)} %get-tuple-element.10.gate_ref, ...), custom_call_target="tpu_custom_call" | custom-call | flops 3449999872 | tf_op jit(solution)/shard_map/attend_last/pallas_call | solution.py:164
  55.5 20.2 %all_to_all.10.got_ref = bf16[16,8,32,128]{3,2,1,0:T(8,128)(2,1)S(1)} all-to-all(bf16[16,8,32,128]{3,2,1,0:T(8,128)(2,1)S(1)} %attend_last.1), channel_id=1, replica_groups={{40,56,20,4,36,8,12,44,52,28,32,16,0,24,60,48},{41,57,21,5,37,9,13,45,5..., dimensions={0} | all-to-all | bytes 2097152 | tf_op jit(solution)/shard_map/all_to_all | solution.py:188
  75.8 1.3 %unpack.1 = bf16[32,128,128]{2,1,0:T(8,128)(2,1)} custom-call(bf16[16,8,32,128]{3,2,1,0:T(8,128)(2,1)S(1)} %all_to_all.10.got_ref), custom_call_target="tpu_custom_call" | custom-call | flops 1150000000 | tf_op jit(solution)/shard_map/unpack/pallas_call | solution.py:164
Async XLA Ops:
  3.8 11.0 %copy-start.7 = (s32[32]{0:T(128)S(1)}, s32[32]{0:T(128)}, u32[]{:S(2)}) copy-start(s32[32]{0:T(128)} %constant.18.clone) | copy-start | bytes 388
  3.8 29.3 %all-to-all-start = ((bf16[16,12,32,128]{3,2,1,0:T(8,128)(2,1)}), bf16[16,12,32,128]{3,2,1,0:T(8,128)(2,1)S(1)}, u32[]{:S(2)}, u32[]{:S(2)}) async-start(bf16[16,12,32,128]{3,2,1,0:T(8,128)(2,1)} %pack.1), calls=%async_computation | async-start | bytes 3145728 | tf_op jit(solution)/shard_map/all_to_all | solution.py:188
  16.1 19.5 %copy-start = (bf16[128,128]{1,0:T(8,128)(2,1)S(1)}, bf16[128,128]{1,0:T(8,128)(2,1)}, u32[]{:S(2)}) copy-start(bf16[128,128]{1,0:T(8,128)(2,1)} %wq_ref.1) | copy-start | bytes 98308
  16.1 19.5 %copy-start.1 = (bf16[128,128]{1,0:T(8,128)(2,1)S(1)}, bf16[128,128]{1,0:T(8,128)(2,1)}, u32[]{:S(2)}) copy-start(bf16[128,128]{1,0:T(8,128)(2,1)} %wk_ref.1) | copy-start | bytes 98308
  16.1 19.5 %copy-start.2 = (bf16[128,128]{1,0:T(8,128)(2,1)S(1)}, bf16[128,128]{1,0:T(8,128)(2,1)}, u32[]{:S(2)}) copy-start(bf16[128,128]{1,0:T(8,128)(2,1)} %wv_ref.1) | copy-start | bytes 98308
  16.1 19.5 %copy-start.3 = (bf16[128,128]{1,0:T(8,128)(2,1)S(1)}, bf16[128,128]{1,0:T(8,128)(2,1)}, u32[]{:S(2)}) copy-start(bf16[128,128]{1,0:T(8,128)(2,1)} %wg_ref.1) | copy-start | bytes 98308
  16.1 19.5 %copy-start.5 = (f32[128]{0:T(128)S(1)}, f32[128]{0:T(128)}, u32[]{:S(2)}) copy-start(f32[128]{0:T(128)} %param.17) | copy-start | bytes 1540
  33.9 5.1 %collective-permute-start.1 = (bf16[4,128,512]{2,1,0:T(8,128)(2,1)S(1)}, bf16[4,128,512]{2,1,0:T(8,128)(2,1)S(1)}, u32[]{:S(2)}, u32[]{:S(2)}) collective-permute-start(bf16[4,128,512]{2,1,0:T(8,128)(2,1)S(1)} %turn_bias.1.refs_0_), channel_id=1, source_target_pairs={{0,1},{1,0},{2,3},{3,2},{4,5},{5,4},{6,7},{7,6},{8,9},{9,8},{10,11... | collective-permute-start | bytes 1572872 | tf_op jit(solution)/shard_map/ppermute | solution.py:205
  34.0 14.3 %collective-permute-start = (bf16[4,128,512]{2,1,0:T(8,128)(2,1)S(1)}, bf16[4,128,512]{2,1,0:T(8,128)(2,1)S(1)}, u32[]{:S(2)}, u32[]{:S(2)}) collective-permute-start(bf16[4,128,512]{2,1,0:T(8,128)(2,1)S(1)} %turn_bias.1.refs_0_), channel_id=1, source_target_pairs={{0,2},{2,0},{1,3},{3,1},{4,6},{6,4},{5,7},{7,5},{8,10},{10,8},{9,1... | collective-permute-start | bytes 1572872 | tf_op jit(solution)/shard_map/ppermute | solution.py:204
  35.6 3.4 %copy-start.4 = (bf16[128,128]{1,0:T(8,128)(2,1)S(1)}, bf16[128,128]{1,0:T(8,128)(2,1)}, u32[]{:S(2)}) copy-start(bf16[128,128]{1,0:T(8,128)(2,1)} %wo_ref.5) | copy-start | bytes 98308
  35.6 3.4 %copy-start.6 = (f32[128]{0:T(128)S(1)}, f32[128]{0:T(128)}, u32[]{:S(2)}) copy-start(f32[128]{0:T(128)} %param.20) | copy-start | bytes 1540
  48.4 3.6 %collective-permute-start.2 = (bf16[4,128,512]{2,1,0:T(8,128)(2,1)S(1)}, bf16[4,128,512]{2,1,0:T(8,128)(2,1)S(1)}, u32[]{:S(2)}, u32[]{:S(2)}) collective-permute-start(bf16[4,128,512]{2,1,0:T(8,128)(2,1)S(1)} %collective-permute-done.refs_0_), channel_id=1, source_target_pairs={{0,1},{1,0},{2,3},{3,2},{4,5},{5,4},{6,7},{7,6},{8,9},{9,8},{10,11... | collective-permute-start | bytes 1572872 | tf_op jit(solution)/shard_map/ppermute | solution.py:226
where the time goes:
time: 77.3 us; the launch traced here: 77 us
  Pallas kernels  22.7 us (29%)
  blocking collectives  20.2 us (26%)
  waiting for transfers between devices  20.1 us (26%)
  starting transfers between devices  12 us (16%)
  local copies, waits for them, and re-layouts  1.28 us (2%)
  between operations  0.78 us (1%)
    pallas_call x7, Pallas kernels, call(): pl.pallas_call(kernel, out_shape=out, scratch_shapes=list(scratch), compi...  22.7 us
    all_to_all x1, blocking collectives, exchange(): lax.all_to_all(array, 'row', 0, 0, axis_index_groups=[list(order)], tiled...  20.2 us
    all_to_all x1, waiting for transfers between devices, exchange(): lax.all_to_all(array, 'row', 0, 0, axis_index_groups=[list(order)], tiled...  17.1 us
    all_to_all x1, starting transfers between devices, exchange(): lax.all_to_all(array, 'row', 0, 0, axis_index_groups=[list(order)], tiled...  10.4 us
    ppermute x1, waiting for transfers between devices, local(): far = lax.ppermute(own, 'xl', swap)  3.04 us
    ppermute x1, starting transfers between devices, local(): far = lax.ppermute(own, 'xl', swap)  1.57 us
  transfers between devices with their start and end apart: 4, of which 2 were waited for; matrix products, arithmetic and copies ran while one was open for 2% of the time, Pallas kernels for 17%

commit v1 on v0

--- a/solution.py
+++ b/solution.py
@@ -60,7 +60,8 @@
 
 
 def project_kernel(
-    info_ref, got_ref, wq_ref, wk_ref, wv_ref, wg_ref, bg_ref, qkv_ref, gate_ref, *, head_size
+    info_ref, got_ref, wq_ref, wk_ref, wv_ref, wg_ref, bg_ref, qkv_ref, gate_ref, even_ref, *,
+    head_size
 ):
     rows, _, tile_rows, channels = got_ref.shape
     picks, tokens = qkv_ref.shape[:2]
@@ -72,16 +73,18 @@
         ).astype(F32)
         projected = jnp.dot(normalize(mine), weights_in, preferred_element_type=F32)
         for q in range(group):
-            real = column_is_real(info_ref, first + q, rows, rows * picks)
-            scale = jnp.where(real, F32(head_size ** (-0.5)), F32(0.0))
             part = projected[q * tokens : (q + 1) * tokens]
-            qkv_ref[first + q, :, :channels] = (part[:, :channels] * scale).astype(BF16)
+            qkv_ref[first + q, :, :channels] = (part[:, :channels] * head_size ** (-0.5)).astype(BF16)
             qkv_ref[first + q, :, channels:] = part[:, channels : 3 * channels].astype(BF16)
+            values = part[:, 2 * channels : 3 * channels].astype(BF16).astype(F32)
+            even_ref[first + q] = jnp.mean(values, axis=0, keepdims=True)
             gate_ref[first + q] = jax.nn.sigmoid(part[:, 3 * channels :] + bg_ref[...])
 
 
-def attend_kernel(info_ref, got_ref, qkv_ref, gate_ref, wo_ref, bo_ref, *refs, far):
-    blocks, out_ref, bias_s = refs[:-2], refs[-2], refs[-1]
+def attend_kernel(
+    info_ref, got_ref, qkv_ref, gate_ref, even_ref, wo_ref, bo_ref, *refs, far
+):
+    blocks, out_ref = refs[:-1], refs[-1]
     core, pair = info_ref[0], info_ref[1]
     earlier, blocks = (blocks[:2], blocks[2:]) if far == 2 else ((), blocks)
     rows, _, tile_rows, channels = got_ref.shape
@@ -90,37 +93,27 @@
     head_size = channels // heads
     tiles = width // tile_rows
     half = 1 - pair if far else pair
-    bias_s[heads] = jnp.zeros(bias_s.shape[1:], F32)
     starts = []
-    for n, block in enumerate(blocks):
-        for h in range(heads):
-            bias_s[h, n * width : (n + 1) * width] = block[h].astype(F32)
+    for n in range(len(blocks)):
         mine = core if (n == 0) == (far != 2) else 1 - core
         starts.append((half * 2 + mine) * width)
     lane_head = lax.broadcasted_iota(jnp.int32, (1, channels), 1) // head_size
     for n, start in enumerate(starts):
         at = pl.ds(pl.multiple_of(start, width), width)
-        attended = []
-        for q in range(picks):
-            real = column_is_real(info_ref, q, rows, width)
+        bias = blocks[n][...].reshape(heads * width, tokens).astype(F32)
+
+        def product(q):
             some = qkv_ref[q, at, :channels]
             keys = qkv_ref[q, :, channels : 2 * channels]
-            values = qkv_ref[q, :, 2 * channels :]
-            values_ones = jnp.concatenate([values, jnp.ones_like(values)], axis=1)
             stacked = jnp.concatenate(
                 [jnp.where(lane_head == h, some, jnp.zeros_like(some)) for h in range(heads)],
                 axis=0,
             )
-            bias = jnp.concatenate(
-                [
-                    bias_s[jnp.where(real, h, heads), n * width : (n + 1) * width]
-                    for h in range(heads)
-                ],
-                axis=0,
-            )
-            scores = lax.dot_general(stacked, keys, CONTRACT_LAST, preferred_element_type=F32)
-            scores = scores + bias
-            weights = jnp.exp(scores - jnp.max(scores, axis=1, keepdims=True)).astype(BF16)
+            return lax.dot_general(stacked, keys, CONTRACT_LAST, preferred_element_type=F32)
+
+        def mixed(q, weights):
+            values = qkv_ref[q, :, 2 * channels :]
+            values_ones = jnp.concatenate([values, jnp.ones_like(values)], axis=1)
             both = jnp.dot(weights, values_ones, preferred_element_type=F32)
             top = total = None
             for h in range(heads):
@@ -130,7 +123,18 @@
                 else:
                     top = jnp.where(lane_head == h, one[:, :channels], top)
                     total = jnp.where(lane_head == h, one[:, channels:], total)
-            attended.append(gate_ref[q, at] * (top / total))
+            real = column_is_real(info_ref, q, rows, width)
+            return gate_ref[q, at] * jnp.where(real, top / total, even_ref[q])
+
+        attended = []
+        following, weights = product(0), None
+        for q in range(picks):
+            scores = following + bias
+            following = product(q + 1) if q + 1 < picks else None
+            if q:
+                attended.append(mixed(q - 1, weights))
+            weights = jnp.exp(scores - jnp.max(scores, axis=1, keepdims=True)).astype(BF16)
+        attended.append(mixed(picks - 1, weights))
         mix = jnp.concatenate(attended, axis=0).astype(BF16)
         update = jnp.dot(mix, wo_ref[...], preferred_element_type=F32) + bo_ref[...]
         for t in range(tiles):
@@ -203,9 +207,12 @@
     own = call(bias_kernel, "turn_bias", of((heads, tile_cols, tokens), BF16), info, got, cost=MICROSECOND)
     far = lax.ppermute(own, "xl", swap)
     near = lax.ppermute(own, "core", swap)
-    qkv, gate = call(
+    qkv, gate, even = call(
         functools.partial(project_kernel, head_size=channels // heads), "project",
-        (of((picks, tokens, 3 * channels), BF16), of((picks, tokens, channels), F32)),
+        (
+            of((picks, tokens, 3 * channels), BF16), of((picks, tokens, channels), F32),
+            of((picks, 1, channels), F32),
+        ),
         info, got, w_query, w_key, w_value, w_gate, b_gate[None],
         cost=3 * MICROSECOND,
     )
@@ -216,9 +223,8 @@
         return call(
             functools.partial(attend_kernel, far=far), name,
             of((tiles, picks, tile_rows, channels), BF16),
-            info, got, qkv, gate, w_out, b_out[None], *earlier, *blocks,
+            info, got, qkv, gate, even, w_out, b_out[None], *earlier, *blocks,
             cost=3 * count * MICROSECOND,
-            scratch=[pltpu.VMEM((heads + 1, count * tile_cols, tokens), F32)],
         )
 
     first = attend("attend_near", 0, own, near)

time: 77.3 us -> 77 us (level)
  no operation moved by 1% of the time
where the time goes in v1:
time: 77 us; the launch traced here: 76.8 us
  Pallas kernels  22.3 us (29%)
  waiting for transfers between devices  20.2 us (26%)
  blocking collectives  20.2 us (26%)
  starting transfers between devices  12 us (16%)
  local copies, waits for them, and re-layouts  1.28 us (2%)
  between operations  0.78 us (1%)
    pallas_call x7, Pallas kernels, call(): pl.pallas_call(kernel, out_shape=out, scratch_shapes=list(scratch), compi...  22.3 us
    all_to_all x1, blocking collectives, exchange(): lax.all_to_all(array, 'row', 0, 0, axis_index_groups=[list(order)], tiled...  20.2 us
    all_to_all x1, waiting for transfers between devices, exchange(): lax.all_to_all(array, 'row', 0, 0, axis_index_groups=[list(order)], tiled...  17.1 us
    all_to_all x1, starting transfers between devices, exchange(): lax.all_to_all(array, 'row', 0, 0, axis_index_groups=[list(order)], tiled...  10.4 us
    ppermute x1, waiting for transfers between devices, local(): far = lax.ppermute(own, 'xl', swap)  3.17 us
    ppermute x1, starting transfers between devices, local(): far = lax.ppermute(own, 'xl', swap)  1.57 us
  transfers between devices with their start and end apart: 4, of which 2 were waited for; matrix products, arithmetic and copies ran while one was open for 2% of the time, Pallas kernels for 17%

profile of v1, /device:TPU:0, one launch (start us, length us, event | category | flops | bytes accessed | tf_op | source)
XLA Modules:
  0.0 76.8 jit_solution(8700977381231629463)
XLA Ops:
  0.0 3.8 %pack.1 = bf16[16,12,32,128]{3,2,1,0:T(8,128)(2,1)} custom-call(bf16[32,128,128]{2,1,0:T(8,128)(2,1)} %x_ref.1, bf16[4,128]{1,0:T(4,128)(2,1)} %bitcast.9), custom_call_target="tpu_custom_call" | custom-call | flops 4600000000 | tf_op jit(solution)/shard_map/pack/pallas_call | solution.py:168
  3.8 0.0 copy-start.7
  3.8 10.4 %all-to-all-start = ((bf16[16,12,32,128]{3,2,1,0:T(8,128)(2,1)}), bf16[16,12,32,128]{3,2,1,0:T(8,128)(2,1)S(1)}, u32[]{:S(2)}, u32[]{:S(2)}) async-start(bf16[16,12,32,128]{3,2,1,0:T(8,128)(2,1)} %pack.1), calls=%async_computation | async-start | bytes 3145728 | tf_op jit(solution)/shard_map/all_to_all | solution.py:192
  14.8 0.0 copy-done.7
  14.8 0.6 dynamic_slice.3
  15.4 0.7 concatenate.3.info_ref
  16.1 0.0 copy-start
  16.1 0.0 copy-start.1
  16.1 0.0 copy-start.2
  16.1 0.0 copy-start.3
  16.1 0.0 copy-start.5
  16.1 17.1 %all-to-all-done.got_ref = bf16[16,12,32,128]{3,2,1,0:T(8,128)(2,1)S(1)} async-done(((bf16[16,12,32,128]{3,2,1,0:T(8,128)(2,1)}), bf16[16,12,32,128]{3,2,1,0:T(8,128)(2,1)S(1)}, u32[]{:S(2)}, u32[]{:S(2)}) %all-to-all-start) | async-done | bytes 1572896 | tf_op jit(solution)/shard_map/all_to_all | solution.py:192
  33.2 0.7 turn_bias.1.refs_0_
  33.9 0.1 collective-permute-start.1
  34.0 1.6 %collective-permute-start = (bf16[4,128,512]{2,1,0:T(8,128)(2,1)S(1)}, bf16[4,128,512]{2,1,0:T(8,128)(2,1)S(1)}, u32[]{:S(2)}, u32[]{:S(2)}) collective-permute-start(bf16[4,128,512]{2,1,0:T(8,128)(2,1)S(1)} %turn_bias.1.refs_0_), channel_id=1, source_target_pairs={{0,2},{2,0},{1,3},{3,1},{4,6},{6,4},{5,7},{7,5},{8,10},{10,8},{9,1... | collective-permute-start | bytes 1572872 | tf_op jit(solution)/shard_map/ppermute | solution.py:208
  35.6 0.0 copy-done
  35.6 0.0 copy-done.1
  35.6 0.0 copy-done.2
  35.6 0.0 copy-done.3
  35.6 0.0 copy-done.5
  35.6 0.0 copy-start.4
  35.6 0.0 copy-start.6
  35.6 3.4 %project.1 = (bf16[8,512,384]{2,1,0:T(8,128)(2,1)S(1)}, f32[8,512,128]{2,1,0:T(8,128)S(1)}, f32[8,1,128]{2,1,0:T(1,128)S(1)}) custom-call(s32[36]{0:T(128)S(1)} %concatenate.3.info_ref, bf16[16,12,32,128]{3,2,1,0:T(8,128)(2,1)S(1)} %all-to-all-done.got_ref, bf16[128,128]{1,0:T(8,128)(2,1)S(1)} %copy-done, bf16[128,128]{1,0:T(8,128)(2,1)S(1)} %copy-done.1, ...), custom_call_target="tpu_custom_call" | custom-call | flops 3449999872 | tf_op jit(solution)/shard_map/project/pallas_call | solution.py:168
  39.0 0.0 collective-permute-done.1.refs_1_
  39.0 0.0 copy-done.4
  39.0 0.0 copy-done.6
  39.0 6.2 %attend_near.1.refs_0_ = bf16[8,8,32,128]{3,2,1,0:T(8,128)(2,1)S(1)} custom-call(s32[36]{0:T(128)S(1)} %concatenate.3.info_ref, bf16[16,12,32,128]{3,2,1,0:T(8,128)(2,1)S(1)} %all-to-all-done.got_ref, bf16[8,512,384]{2,1,0:T(8,128)(2,1)S(1)} %get-tuple-element.10.qkv_ref, f32[8,512,128]{2,1,0:T(8,128)S(1)} %get-tuple-element.11.gate_ref, ...), custom_call_target="tpu_custom_call" | custom-call | flops 6899999744 | tf_op jit(solution)/shard_map/attend_near/pallas_call | solution.py:168
  45.2 3.2 %collective-permute-done.refs_0_ = bf16[4,128,512]{2,1,0:T(8,128)(2,1)S(1)} collective-permute-done((bf16[4,128,512]{2,1,0:T(8,128)(2,1)S(1)}, bf16[4,128,512]{2,1,0:T(8,128)(2,1)S(1)}, u32[]{:S(2)}, u32[]{:S(2)}) %collective-permute-start) | collective-permute-done | bytes 524320 | tf_op jit(solution)/shard_map/ppermute | solution.py:208
  48.4 0.0 collective-permute-start.2
  48.4 3.4 %attend_far.1.refs_1_ = bf16[4,8,32,128]{3,2,1,0:T(8,128)(2,1)S(1)} custom-call(s32[36]{0:T(128)S(1)} %concatenate.3.info_ref, bf16[16,12,32,128]{3,2,1,0:T(8,128)(2,1)S(1)} %all-to-all-done.got_ref, bf16[8,512,384]{2,1,0:T(8,128)(2,1)S(1)} %get-tuple-element.10.qkv_ref, f32[8,512,128]{2,1,0:T(8,128)S(1)} %get-tuple-element.11.gate_ref, ...), custom_call_target="tpu_custom_call" | custom-call | flops 3449999872 | tf_op jit(solution)/shard_map/attend_far/pallas_call | solution.py:168
  51.8 0.0 collective-permute-done.2.refs_2_
  51.8 3.5 %attend_last.1 = bf16[16,8,32,128]{3,2,1,0:T(8,128)(2,1)S(1)} custom-call(s32[36]{0:T(128)S(1)} %concatenate.3.info_ref, bf16[16,12,32,128]{3,2,1,0:T(8,128)(2,1)S(1)} %all-to-all-done.got_ref, bf16[8,512,384]{2,1,0:T(8,128)(2,1)S(1)} %get-tuple-element.10.qkv_ref, f32[8,512,128]{2,1,0:T(8,128)S(1)} %get-tuple-element.11.gate_ref, ...), custom_call_target="tpu_custom_call" | custom-call | flops 3449999872 | tf_op jit(solution)/shard_map/attend_last/pallas_call | solution.py:168
  55.3 20.2 %all_to_all.10.got_ref = bf16[16,8,32,128]{3,2,1,0:T(8,128)(2,1)S(1)} all-to-all(bf16[16,8,32,128]{3,2,1,0:T(8,128)(2,1)S(1)} %attend_last.1), channel_id=1, replica_groups={{40,56,20,4,36,8,12,44,52,28,32,16,0,24,60,48},{41,57,21,5,37,9,13,45,5..., dimensions={0} | all-to-all | bytes 2097152 | tf_op jit(solution)/shard_map/all_to_all | solution.py:192
  75.5 1.3 %unpack.1 = bf16[32,128,128]{2,1,0:T(8,128)(2,1)} custom-call(bf16[16,8,32,128]{3,2,1,0:T(8,128)(2,1)S(1)} %all_to_all.10.got_ref), custom_call_target="tpu_custom_call" | custom-call | flops 1150000000 | tf_op jit(solution)/shard_map/unpack/pallas_call | solution.py:168
Async XLA Ops:
  3.8 11.0 %copy-start.7 = (s32[32]{0:T(128)S(1)}, s32[32]{0:T(128)}, u32[]{:S(2)}) copy-start(s32[32]{0:T(128)} %constant.18.clone) | copy-start | bytes 388
  3.8 29.3 %all-to-all-start = ((bf16[16,12,32,128]{3,2,1,0:T(8,128)(2,1)}), bf16[16,12,32,128]{3,2,1,0:T(8,128)(2,1)S(1)}, u32[]{:S(2)}, u32[]{:S(2)}) async-start(bf16[16,12,32,128]{3,2,1,0:T(8,128)(2,1)} %pack.1), calls=%async_computation | async-start | bytes 3145728 | tf_op jit(solution)/shard_map/all_to_all | solution.py:192
  16.1 19.5 %copy-start = (bf16[128,128]{1,0:T(8,128)(2,1)S(1)}, bf16[128,128]{1,0:T(8,128)(2,1)}, u32[]{:S(2)}) copy-start(bf16[128,128]{1,0:T(8,128)(2,1)} %wq_ref.1) | copy-start | bytes 98308
  16.1 19.5 %copy-start.1 = (bf16[128,128]{1,0:T(8,128)(2,1)S(1)}, bf16[128,128]{1,0:T(8,128)(2,1)}, u32[]{:S(2)}) copy-start(bf16[128,128]{1,0:T(8,128)(2,1)} %wk_ref.1) | copy-start | bytes 98308
  16.1 19.5 %copy-start.2 = (bf16[128,128]{1,0:T(8,128)(2,1)S(1)}, bf16[128,128]{1,0:T(8,128)(2,1)}, u32[]{:S(2)}) copy-start(bf16[128,128]{1,0:T(8,128)(2,1)} %wv_ref.1) | copy-start | bytes 98308
  16.1 19.5 %copy-start.3 = (bf16[128,128]{1,0:T(8,128)(2,1)S(1)}, bf16[128,128]{1,0:T(8,128)(2,1)}, u32[]{:S(2)}) copy-start(bf16[128,128]{1,0:T(8,128)(2,1)} %wg_ref.1) | copy-start | bytes 98308
  16.1 19.5 %copy-start.5 = (f32[128]{0:T(128)S(1)}, f32[128]{0:T(128)}, u32[]{:S(2)}) copy-start(f32[128]{0:T(128)} %param.17) | copy-start | bytes 1540
  33.9 5.1 %collective-permute-start.1 = (bf16[4,128,512]{2,1,0:T(8,128)(2,1)S(1)}, bf16[4,128,512]{2,1,0:T(8,128)(2,1)S(1)}, u32[]{:S(2)}, u32[]{:S(2)}) collective-permute-start(bf16[4,128,512]{2,1,0:T(8,128)(2,1)S(1)} %turn_bias.1.refs_0_), channel_id=1, source_target_pairs={{0,1},{1,0},{2,3},{3,2},{4,5},{5,4},{6,7},{7,6},{8,9},{9,8},{10,11... | collective-permute-start | bytes 1572872 | tf_op jit(solution)/shard_map/ppermute | solution.py:209
  34.0 14.3 %collective-permute-start = (bf16[4,128,512]{2,1,0:T(8,128)(2,1)S(1)}, bf16[4,128,512]{2,1,0:T(8,128)(2,1)S(1)}, u32[]{:S(2)}, u32[]{:S(2)}) collective-permute-start(bf16[4,128,512]{2,1,0:T(8,128)(2,1)S(1)} %turn_bias.1.refs_0_), channel_id=1, source_target_pairs={{0,2},{2,0},{1,3},{3,1},{4,6},{6,4},{5,7},{7,5},{8,10},{10,8},{9,1... | collective-permute-start | bytes 1572872 | tf_op jit(solution)/shard_map/ppermute | solution.py:208
  35.6 3.4 %copy-start.4 = (bf16[128,128]{1,0:T(8,128)(2,1)S(1)}, bf16[128,128]{1,0:T(8,128)(2,1)}, u32[]{:S(2)}) copy-start(bf16[128,128]{1,0:T(8,128)(2,1)} %wo_ref.5) | copy-start | bytes 98308
  35.6 3.4 %copy-start.6 = (f32[128]{0:T(128)S(1)}, f32[128]{0:T(128)}, u32[]{:S(2)}) copy-start(f32[128]{0:T(128)} %param.20) | copy-start | bytes 1540
  48.4 3.4 %collective-permute-start.2 = (bf16[4,128,512]{2,1,0:T(8,128)(2,1)S(1)}, bf16[4,128,512]{2,1,0:T(8,128)(2,1)S(1)}, u32[]{:S(2)}, u32[]{:S(2)}) collective-permute-start(bf16[4,128,512]{2,1,0:T(8,128)(2,1)S(1)} %collective-permute-done.refs_0_), channel_id=1, source_target_pairs={{0,1},{1,0},{2,3},{3,2},{4,5},{5,4},{6,7},{7,6},{8,9},{9,8},{10,11... | collective-permute-start | bytes 1572872 | tf_op jit(solution)/shard_map/ppermute | solution.py:232

commit v2 on v1

--- a/solution.py
+++ b/solution.py
@@ -50,8 +50,8 @@
     first = got_ref.shape[1] - heads
     key_ok = lax.broadcasted_iota(jnp.int32, (1, tokens), 1) < info_ref[3]
     for h in range(heads):
-        block = jnp.concatenate([got_ref[at, first + h] for at in PLACE], axis=0).astype(F32)
-        out_ref[h] = jnp.where(key_ok, jnp.transpose(block), MASKED_SCORE).astype(BF16)
+        block = jnp.transpose(jnp.concatenate([got_ref[at, first + h] for at in PLACE], axis=0))
+        out_ref[h] = jnp.where(key_ok, block.astype(F32), MASKED_SCORE).astype(BF16)
 
 
 def column_is_real(info_ref, q, peers, width):
@@ -233,7 +233,13 @@
     second = attend("attend_far", 1, far)
     done = attend("attend_last", 2, last, earlier=(first, second))
     back = exchange(done, ORDER_BACK)
-    return call(unpack_kernel, "unpack", of(pair_state.shape, BF16), back, cost=MICROSECOND)
+    return call(
+        unpack_kernel, "unpack", of(pair_state.shape, BF16), back,
+        grid=(2,),
+        in_specs=[pl.BlockSpec((peers, picks, part, channels), lambda a: (0, 0, a, 0))],
+        out_specs=pl.BlockSpec((part, tile_cols, channels), lambda a: (a, 0, 0)),
+        cost=MICROSECOND,
+    )
 
 
 def solution(mesh):

time: 77 us -> 77 us (level)
  no operation moved by 1% of the time
where the time goes in v2:
time: 77 us; the launch traced here: 76.7 us
  Pallas kernels  22.2 us (29%)
  waiting for transfers between devices  20.2 us (26%)
  blocking collectives  20.2 us (26%)
  starting transfers between devices  12 us (16%)
  local copies, waits for them, and re-layouts  1.28 us (2%)
  between operations  0.78 us (1%)
    pallas_call x7, Pallas kernels, call(): pl.pallas_call(kernel, out_shape=out, scratch_shapes=list(scratch), compi...  22.2 us
    all_to_all x1, blocking collectives, exchange(): lax.all_to_all(array, 'row', 0, 0, axis_index_groups=[list(order)], tiled...  20.2 us
    all_to_all x1, waiting for transfers between devices, exchange(): lax.all_to_all(array, 'row', 0, 0, axis_index_groups=[list(order)], tiled...  17.1 us
    all_to_all x1, starting transfers between devices, exchange(): lax.all_to_all(array, 'row', 0, 0, axis_index_groups=[list(order)], tiled...  10.4 us
    ppermute x1, waiting for transfers between devices, local(): far = lax.ppermute(own, 'xl', swap)  3.17 us
    ppermute x1, starting transfers between devices, local(): far = lax.ppermute(own, 'xl', swap)  1.57 us
  transfers between devices with their start and end apart: 4, of which 2 were waited for; matrix products, arithmetic and copies ran while one was open for 2% of the time, Pallas kernels for 17%

profile of v2, /device:TPU:0, one launch (start us, length us, event | category | flops | bytes accessed | tf_op | source)
XLA Modules:
  0.0 76.7 jit_solution(3372982543788636839)
XLA Ops:
  0.0 3.8 %pack.1 = bf16[16,12,32,128]{3,2,1,0:T(8,128)(2,1)} custom-call(bf16[32,128,128]{2,1,0:T(8,128)(2,1)} %x_ref.1, bf16[4,128]{1,0:T(4,128)(2,1)} %bitcast.9), custom_call_target="tpu_custom_call" | custom-call | flops 4600000000 | tf_op jit(solution)/shard_map/pack/pallas_call | solution.py:168
  3.8 0.0 copy-start.7
  3.8 10.4 %all-to-all-start = ((bf16[16,12,32,128]{3,2,1,0:T(8,128)(2,1)}), bf16[16,12,32,128]{3,2,1,0:T(8,128)(2,1)S(1)}, u32[]{:S(2)}, u32[]{:S(2)}) async-start(bf16[16,12,32,128]{3,2,1,0:T(8,128)(2,1)} %pack.1), calls=%async_computation | async-start | bytes 3145728 | tf_op jit(solution)/shard_map/all_to_all | solution.py:192
  14.8 0.0 copy-done.7
  14.8 0.6 dynamic_slice.3
  15.4 0.7 concatenate.3.info_ref
  16.1 0.0 copy-start
  16.1 0.0 copy-start.1
  16.1 0.0 copy-start.2
  16.1 0.0 copy-start.3
  16.1 0.0 copy-start.5
  16.1 17.1 %all-to-all-done.got_ref = bf16[16,12,32,128]{3,2,1,0:T(8,128)(2,1)S(1)} async-done(((bf16[16,12,32,128]{3,2,1,0:T(8,128)(2,1)}), bf16[16,12,32,128]{3,2,1,0:T(8,128)(2,1)S(1)}, u32[]{:S(2)}, u32[]{:S(2)}) %all-to-all-start) | async-done | bytes 1572896 | tf_op jit(solution)/shard_map/all_to_all | solution.py:192
  33.2 0.7 turn_bias.1.refs_0_
  33.9 0.1 collective-permute-start.1
  34.0 1.6 %collective-permute-start = (bf16[4,128,512]{2,1,0:T(8,128)(2,1)S(1)}, bf16[4,128,512]{2,1,0:T(8,128)(2,1)S(1)}, u32[]{:S(2)}, u32[]{:S(2)}) collective-permute-start(bf16[4,128,512]{2,1,0:T(8,128)(2,1)S(1)} %turn_bias.1.refs_0_), channel_id=1, source_target_pairs={{0,2},{2,0},{1,3},{3,1},{4,6},{6,4},{5,7},{7,5},{8,10},{10,8},{9,1... | collective-permute-start | bytes 1572872 | tf_op jit(solution)/shard_map/ppermute | solution.py:208
  35.6 0.0 copy-done
  35.6 0.0 copy-done.1
  35.6 0.0 copy-done.2
  35.6 0.0 copy-done.3
  35.6 0.0 copy-done.5
  35.6 0.0 copy-start.4
  35.6 0.0 copy-start.6
  35.6 3.4 %project.1 = (bf16[8,512,384]{2,1,0:T(8,128)(2,1)S(1)}, f32[8,512,128]{2,1,0:T(8,128)S(1)}, f32[8,1,128]{2,1,0:T(1,128)S(1)}) custom-call(s32[36]{0:T(128)S(1)} %concatenate.3.info_ref, bf16[16,12,32,128]{3,2,1,0:T(8,128)(2,1)S(1)} %all-to-all-done.got_ref, bf16[128,128]{1,0:T(8,128)(2,1)S(1)} %copy-done, bf16[128,128]{1,0:T(8,128)(2,1)S(1)} %copy-done.1, ...), custom_call_target="tpu_custom_call" | custom-call | flops 3449999872 | tf_op jit(solution)/shard_map/project/pallas_call | solution.py:168
  39.0 0.0 collective-permute-done.1.refs_1_
  39.0 0.0 copy-done.4
  39.0 0.0 copy-done.6
  39.0 6.2 %attend_near.1.refs_0_ = bf16[8,8,32,128]{3,2,1,0:T(8,128)(2,1)S(1)} custom-call(s32[36]{0:T(128)S(1)} %concatenate.3.info_ref, bf16[16,12,32,128]{3,2,1,0:T(8,128)(2,1)S(1)} %all-to-all-done.got_ref, bf16[8,512,384]{2,1,0:T(8,128)(2,1)S(1)} %get-tuple-element.10.qkv_ref, f32[8,512,128]{2,1,0:T(8,128)S(1)} %get-tuple-element.11.gate_ref, ...), custom_call_target="tpu_custom_call" | custom-call | flops 6899999744 | tf_op jit(solution)/shard_map/attend_near/pallas_call | solution.py:168
  45.2 3.2 %collective-permute-done.refs_0_ = bf16[4,128,512]{2,1,0:T(8,128)(2,1)S(1)} collective-permute-done((bf16[4,128,512]{2,1,0:T(8,128)(2,1)S(1)}, bf16[4,128,512]{2,1,0:T(8,128)(2,1)S(1)}, u32[]{:S(2)}, u32[]{:S(2)}) %collective-permute-start) | collective-permute-done | bytes 524320 | tf_op jit(solution)/shard_map/ppermute | solution.py:208
  48.3 0.0 collective-permute-start.2
  48.3 3.4 %attend_far.1.refs_1_ = bf16[4,8,32,128]{3,2,1,0:T(8,128)(2,1)S(1)} custom-call(s32[36]{0:T(128)S(1)} %concatenate.3.info_ref, bf16[16,12,32,128]{3,2,1,0:T(8,128)(2,1)S(1)} %all-to-all-done.got_ref, bf16[8,512,384]{2,1,0:T(8,128)(2,1)S(1)} %get-tuple-element.10.qkv_ref, f32[8,512,128]{2,1,0:T(8,128)S(1)} %get-tuple-element.11.gate_ref, ...), custom_call_target="tpu_custom_call" | custom-call | flops 3449999872 | tf_op jit(solution)/shard_map/attend_far/pallas_call | solution.py:168
  51.8 0.0 collective-permute-done.2.refs_2_
  51.8 3.5 %attend_last.1 = bf16[16,8,32,128]{3,2,1,0:T(8,128)(2,1)S(1)} custom-call(s32[36]{0:T(128)S(1)} %concatenate.3.info_ref, bf16[16,12,32,128]{3,2,1,0:T(8,128)(2,1)S(1)} %all-to-all-done.got_ref, bf16[8,512,384]{2,1,0:T(8,128)(2,1)S(1)} %get-tuple-element.10.qkv_ref, f32[8,512,128]{2,1,0:T(8,128)S(1)} %get-tuple-element.11.gate_ref, ...), custom_call_target="tpu_custom_call" | custom-call | flops 3449999872 | tf_op jit(solution)/shard_map/attend_last/pallas_call | solution.py:168
  55.3 20.2 %all_to_all.10.got_ref = bf16[16,8,32,128]{3,2,1,0:T(8,128)(2,1)S(1)} all-to-all(bf16[16,8,32,128]{3,2,1,0:T(8,128)(2,1)S(1)} %attend_last.1), channel_id=1, replica_groups={{40,56,20,4,36,8,12,44,52,28,32,16,0,24,60,48},{41,57,21,5,37,9,13,45,5..., dimensions={0} | all-to-all | bytes 2097152 | tf_op jit(solution)/shard_map/all_to_all | solution.py:192
  75.5 1.2 %unpack.1 = bf16[32,128,128]{2,1,0:T(8,128)(2,1)} custom-call(bf16[16,8,32,128]{3,2,1,0:T(8,128)(2,1)S(1)} %all_to_all.10.got_ref), custom_call_target="tpu_custom_call" | custom-call | flops 1150000000 | tf_op jit(solution)/shard_map/unpack/pallas_call | solution.py:168
Async XLA Ops:
  3.8 11.0 %copy-start.7 = (s32[32]{0:T(128)S(1)}, s32[32]{0:T(128)}, u32[]{:S(2)}) copy-start(s32[32]{0:T(128)} %constant.18.clone) | copy-start | bytes 388
  3.8 29.3 %all-to-all-start = ((bf16[16,12,32,128]{3,2,1,0:T(8,128)(2,1)}), bf16[16,12,32,128]{3,2,1,0:T(8,128)(2,1)S(1)}, u32[]{:S(2)}, u32[]{:S(2)}) async-start(bf16[16,12,32,128]{3,2,1,0:T(8,128)(2,1)} %pack.1), calls=%async_computation | async-start | bytes 3145728 | tf_op jit(solution)/shard_map/all_to_all | solution.py:192
  16.1 19.5 %copy-start = (bf16[128,128]{1,0:T(8,128)(2,1)S(1)}, bf16[128,128]{1,0:T(8,128)(2,1)}, u32[]{:S(2)}) copy-start(bf16[128,128]{1,0:T(8,128)(2,1)} %wq_ref.1) | copy-start | bytes 98308
  16.1 19.5 %copy-start.1 = (bf16[128,128]{1,0:T(8,128)(2,1)S(1)}, bf16[128,128]{1,0:T(8,128)(2,1)}, u32[]{:S(2)}) copy-start(bf16[128,128]{1,0:T(8,128)(2,1)} %wk_ref.1) | copy-start | bytes 98308
  16.1 19.5 %copy-start.2 = (bf16[128,128]{1,0:T(8,128)(2,1)S(1)}, bf16[128,128]{1,0:T(8,128)(2,1)}, u32[]{:S(2)}) copy-start(bf16[128,128]{1,0:T(8,128)(2,1)} %wv_ref.1) | copy-start | bytes 98308
  16.1 19.5 %copy-start.3 = (bf16[128,128]{1,0:T(8,128)(2,1)S(1)}, bf16[128,128]{1,0:T(8,128)(2,1)}, u32[]{:S(2)}) copy-start(bf16[128,128]{1,0:T(8,128)(2,1)} %wg_ref.1) | copy-start | bytes 98308
  16.1 19.5 %copy-start.5 = (f32[128]{0:T(128)S(1)}, f32[128]{0:T(128)}, u32[]{:S(2)}) copy-start(f32[128]{0:T(128)} %param.17) | copy-start | bytes 1540
  33.9 5.1 %collective-permute-start.1 = (bf16[4,128,512]{2,1,0:T(8,128)(2,1)S(1)}, bf16[4,128,512]{2,1,0:T(8,128)(2,1)S(1)}, u32[]{:S(2)}, u32[]{:S(2)}) collective-permute-start(bf16[4,128,512]{2,1,0:T(8,128)(2,1)S(1)} %turn_bias.1.refs_0_), channel_id=1, source_target_pairs={{0,1},{1,0},{2,3},{3,2},{4,5},{5,4},{6,7},{7,6},{8,9},{9,8},{10,11... | collective-permute-start | bytes 1572872 | tf_op jit(solution)/shard_map/ppermute | solution.py:209
  34.0 14.3 %collective-permute-start = (bf16[4,128,512]{2,1,0:T(8,128)(2,1)S(1)}, bf16[4,128,512]{2,1,0:T(8,128)(2,1)S(1)}, u32[]{:S(2)}, u32[]{:S(2)}) collective-permute-start(bf16[4,128,512]{2,1,0:T(8,128)(2,1)S(1)} %turn_bias.1.refs_0_), channel_id=1, source_target_pairs={{0,2},{2,0},{1,3},{3,1},{4,6},{6,4},{5,7},{7,5},{8,10},{10,8},{9,1... | collective-permute-start | bytes 1572872 | tf_op jit(solution)/shard_map/ppermute | solution.py:208
  35.6 3.4 %copy-start.4 = (bf16[128,128]{1,0:T(8,128)(2,1)S(1)}, bf16[128,128]{1,0:T(8,128)(2,1)}, u32[]{:S(2)}) copy-start(bf16[128,128]{1,0:T(8,128)(2,1)} %wo_ref.5) | copy-start | bytes 98308
  35.6 3.4 %copy-start.6 = (f32[128]{0:T(128)S(1)}, f32[128]{0:T(128)}, u32[]{:S(2)}) copy-start(f32[128]{0:T(128)} %param.20) | copy-start | bytes 1540
  48.3 3.4 %collective-permute-start.2 = (bf16[4,128,512]{2,1,0:T(8,128)(2,1)S(1)}, bf16[4,128,512]{2,1,0:T(8,128)(2,1)S(1)}, u32[]{:S(2)}, u32[]{:S(2)}) collective-permute-start(bf16[4,128,512]{2,1,0:T(8,128)(2,1)S(1)} %collective-permute-done.refs_0_), channel_id=1, source_target_pairs={{0,1},{1,0},{2,3},{3,2},{4,5},{5,4},{6,7},{7,6},{8,9},{9,8},{10,11... | collective-permute-start | bytes 1572872 | tf_op jit(solution)/shard_map/ppermute | solution.py:232
